TPU v7x, 32 devices: a whole 2x2x4 slice. The times are simulated.
32 devices in a mesh: dom: 16 (over z, y, core), sub: 2 (over x).
Axes of the slice: x: 2, y: 2, z: 4, core: 2. Of those that a mesh axis runs over, the one named last changes fastest.
Arguments:
- fields: float32 [6, 56, 8192], P(None, None, ('dom', 'sub')), may hold values from -6 to 6
- metric: float32 [9, 8192], P(None, ('dom', 'sub')), may hold values from -4 to 4
- face_geom: float32 [4, 4, 8192], P(None, None, ('dom', 'sub')), as said below
- jacobian_ratio: float32 [56, 8192], P(None, ('dom', 'sub')), may hold values from 0.5 to 2
- curved: int32 [8192], P(('dom', 'sub')), may hold values 0 or 1
- derivatives: float32 [3, 56, 56], replicated, may hold values from -0.75 to 0.75
- lift_matrix: float32 [56, 84], replicated, may hold values from -0.625 to 0.625
- live_count: int32 [32], P(('dom', 'sub')), may hold values from 128 to 256, as said below
- send_list: int32 [32, 3, 2, 32], P(('dom', 'sub')), may hold values from 0 to 1023, as said below
- face_source: int32 [4, 8192], P(None, ('dom', 'sub')), may hold values from 0 to 1215, as said below
- face_permutation: int32 [4, 8192], P(None, ('dom', 'sub')), may hold values from 0 to 5
Outputs:
- advanced: float32 [6, 56, 8192], P(None, None, ('dom', 'sub'))
- section_register: float32 [6, 56, 8192], P(None, None, ('dom', 'sub'))
Inputs may be any that keep to these rules, and one draw needn't show every extreme that they name: `live_count`: some device owns exactly 256 elements. `send_list`: each entry names a face f * 256 + e of an element that its device owns. `face_source`: an entry below 1024 names a face of an owned element of the same device; a larger entry names a ghost slot, never one whose source group lies outside the mesh. `face_geom`: unit normals and a positive surface scale.
All inputs are finite; a program needn't handle non-finite values. No bound on the sum of `curved` on one device may be relied on, other than what follows from the above.
Results may differ from a plain program's by a relative error of at most 0.0003.
Values sent between devices are 32-bit elements; how exact they have to be, the bound alone decides.
A program may use at most 128 MiB of HBM per device.

v0:
```python
import functools

import jax
import jax.numpy as jnp
import numpy as np
from jax import lax
from jax.experimental import pallas as pl
from jax.experimental.pallas import tpu as pltpu
from jax.sharding import PartitionSpec as P

RK_A = (0.0, -567301805773.0 / 1357537059087.0)
RK_B = (1432997174477.0 / 9575080441755.0, 5161836677717.0 / 13612068292357.0)
TIME_STEP = 0.5
SYMMETRIES = ((0, 1, 2), (1, 2, 0), (2, 0, 1), (0, 2, 1), (2, 1, 0), (1, 0, 2))
F32 = jnp.float32
BF16 = jnp.bfloat16
NODES = 56
TRACE = 21
ROWS = 24
GROUP = 3 * ROWS
PAIR = 2 * GROUP
LANES = 128
MESH = pl.DeviceIdType.MESH


def node_tables():
    volume_nodes = [(i, j, k) for i in range(6) for j in range(6 - i) for k in range(6 - i - j)]
    volume_index = {v: n for n, v in enumerate(volume_nodes)}
    triangle = [(a, b) for a in range(6) for b in range(6 - a)]
    triangle_index = {t: n for n, t in enumerate(triangle)}
    face_nodes = np.array(
        [
            [volume_index[a, b, 0] for a, b in triangle],
            [volume_index[a, 0, b] for a, b in triangle],
            [volume_index[a, b, 5 - a - b] for a, b in triangle],
            [volume_index[0, a, b] for a, b in triangle],
        ],
        np.int32,
    )
    permuted = np.array(
        [
            [triangle_index[(a, b, 5 - a - b)[q[0]], (a, b, 5 - a - b)[q[1]]] for a, b in triangle]
            for q in SYMMETRIES
        ],
        np.int32,
    )
    return (face_nodes, permuted)


def zero_one_matrices():
    face_nodes, permuted = node_tables()
    pick = np.zeros((4 * ROWS, NODES), np.float32)
    spread = np.zeros((4 * TRACE, 4 * ROWS), np.float32)
    for f in range(4):
        for m in range(TRACE):
            pick[f * ROWS + m, face_nodes[f, m]] = 1
            spread[f * TRACE + m, f * ROWS + m] = 1
    turn = np.zeros((5 * GROUP, PAIR), np.float32)
    for p in range(1, 6):
        for c in range(3):
            for m in range(TRACE):
                for part in range(2):
                    turn[(p - 1) * GROUP + c * ROWS + m, part * GROUP + c * ROWS + permuted[p, m]] = 1
    pack = np.zeros((2 * PAIR, LANES), np.float32)
    unpack = np.zeros((2 * GROUP, LANES), np.float32)
    for q in range(2):
        for c in range(3):
            for m in range(TRACE):
                lane = (3 * q + c) * TRACE + m
                unpack[q * GROUP + c * ROWS + m, lane] = 1
                for part in range(2):
                    pack[q * PAIR + part * GROUP + c * ROWS + m, lane] = 1
    return tuple(jnp.asarray(a, BF16) for a in (pick, spread, turn, pack, unpack))


def halves(x):
    high = x.astype(BF16)
    low = (x - high.astype(F32)).astype(BF16)
    return high, low


def dot(a, b):
    return jnp.dot(a, b, preferred_element_type=F32)


def dot_nt(a, b):
    return lax.dot_general(a, b, (((1,), (1,)), ((), ())), preferred_element_type=F32)


def lifted(lift, high, low):
    main = dot(lift, high)
    return main[:NODES] + (main[NODES:] + dot(lift, low)[:NODES])


def kernel(
    n_dom,
    n_sub,
    live_ref,
    fields_hbm,
    send_hbm,
    pick_hbm,
    pack_hbm,
    source_hbm,
    deriv_hbm,
    metric_hbm,
    curved_hbm,
    ratio_hbm,
    unpack_hbm,
    turn_hbm,
    perm_hbm,
    geom_hbm,
    lift_hbm,
    spread_hbm,
    adv_ref,
    reg_ref,
    volume,
    scale,
    flux_high,
    flux_low,
    lift_ref,
    send_ref,
    pick_ref,
    pack_ref,
    source_ref,
    deriv_ref,
    metric_ref,
    curved_ref,
    ratio_ref,
    unpack_ref,
    turn_ref,
    perm_ref,
    geom_ref,
    lift_raw,
    spread_ref,
    table,
    inner,
    gathered,
    hot_local,
    hot_ghost,
    hot_send,
    out_buf,
    ghost,
    load_sem,
    send_sem,
    recv_sem,
):
    loads = [
        pltpu.make_async_copy(src, dst, load_sem.at[i])
        for i, (src, dst) in enumerate(
            (
                (fields_hbm, adv_ref),
                (send_hbm, send_ref),
                (pick_hbm, pick_ref),
                (pack_hbm, pack_ref),
                (source_hbm, source_ref),
                (deriv_hbm, deriv_ref),
                (metric_hbm, metric_ref),
                (curved_hbm, curved_ref),
                (ratio_hbm, ratio_ref),
                (unpack_hbm, unpack_ref),
                (turn_hbm, turn_ref),
                (perm_hbm, perm_ref),
                (geom_hbm, geom_ref),
                (lift_hbm, lift_raw),
                (spread_hbm, spread_ref),
            )
        )
    ]
    for load in loads:
        load.start()
    elements = adv_ref.shape[2]
    faces = 4 * elements
    cap = send_ref.shape[2]
    slots = 3 * n_sub * cap
    g = lax.axis_index("dom")
    me = lax.axis_index("sub")
    below = g > 0
    above = g < n_dom - 1
    send_ok = (below, None, above)
    recv_ok = (above, None, below)

    def guarded(ok, act):
        if ok is None:
            act()
        else:
            pl.when(ok)(act)

    def peers(o):
        return [lax.rem(me + d, n_sub) for d in range(1 if o == 1 else 0, n_sub)]

    def rows(o, j):
        return pl.ds(pl.multiple_of((o * n_sub + j) * cap, cap), cap)

    barrier = pltpu.get_barrier_semaphore()
    for o in range(3):

        def greet(o=o):
            for j in peers(o):
                pl.semaphore_signal(barrier, inc=1, device_id=(g + o - 1, j), device_id_type=MESH)

        guarded(send_ok[o], greet)

    def copy(step, o, j):
        return pltpu.make_async_remote_copy(
            src_ref=out_buf.at[step, rows(o, j)],
            dst_ref=ghost.at[step, rows(o, me)],
            send_sem=send_sem.at[step, o, j],
            recv_sem=recv_sem.at[step, o, me],
            device_id=(g + o - 1, j),
            device_id_type=MESH,
        )

    def arrival(step, o, j):
        return pltpu.make_async_remote_copy(
            src_ref=out_buf.at[step, rows(o, j)],
            dst_ref=ghost.at[step, rows(o, j)],
            send_sem=send_sem.at[step, o, j],
            recv_sem=recv_sem.at[step, o, j],
            device_id=(g - o + 1, j),
            device_id_type=MESH,
        )

    loads[1].wait()
    square_r = lax.broadcasted_iota(jnp.int32, (cap, cap), 0)
    square_c = lax.broadcasted_iota(jnp.int32, (cap, cap), 1)
    face_lane = lax.broadcasted_iota(jnp.int32, (cap, faces), 1)
    for o in range(3):
        for j in range(n_sub):
            row = send_ref[o, j : j + 1, :]
            column = jnp.sum(jnp.where(square_r == square_c, row, 0), axis=1, keepdims=True)
            at = (o * n_sub + j) * cap
            hot_send[at : at + cap, :] = jnp.where(face_lane == column, 1.0, 0.0).astype(BF16)

    for load in (loads[0], loads[2], loads[3]):
        load.wait()
    alive = lax.broadcasted_iota(jnp.int32, (1, elements), 1) < live_ref[0]

    for step in range(2):
        parts = []
        for c in range(6):
            if step == 0:
                u = jnp.where(alive, adv_ref[c], 0.0)
                adv_ref[c] = u
            else:
                u = adv_ref[c]
            parts.append(halves(u))
        pick = pick_ref[...]
        for q in range(2):
            high = [dot(pick, parts[3 * q + c][0]) for c in range(3)]
            low = [dot(pick, parts[3 * q + c][1]) for c in range(3)]
            for f in range(4):
                at = f * ROWS
                h = jnp.concatenate([x[at : at + ROWS] for x in high], axis=0)
                l = jnp.concatenate([x[at : at + ROWS] for x in low], axis=0)
                inner[q, f] = h + l
                table[q * PAIR : (q + 1) * PAIR, f * elements : (f + 1) * elements] = jnp.concatenate(
                    [h, l], axis=0
                ).astype(BF16)
        outgoing = dot_nt(hot_send[...], table[...])
        out_buf[step] = dot(outgoing.astype(BF16), pack_ref[...])

        if step == 0:
            for k in range(2):

                def blank_above(k=k):
                    ghost[k, 0 : n_sub * cap, :] = jnp.zeros((n_sub * cap, LANES), F32)

                def blank_below(k=k):
                    ghost[k, 2 * n_sub * cap :, :] = jnp.zeros((n_sub * cap, LANES), F32)

                pl.when(jnp.logical_not(above))(blank_above)
                pl.when(jnp.logical_not(below))(blank_below)
            sides = jnp.minimum(g, 1) + jnp.minimum(n_dom - 1 - g, 1)
            pl.semaphore_wait(barrier, n_sub * (sides + 1) - 1)
        for o in (2, 0, 1):

            def start(o=o):
                for j in peers(o):
                    copy(step, o, j).start()

            guarded(send_ok[o], start)
        ghost[step, rows(1, me), :] = out_buf[step, rows(1, me), :]

        if step == 0:
            for load in loads[4:]:
                load.wait()
            local_row = lax.broadcasted_iota(jnp.int32, (faces, elements), 0)
            ghost_row = lax.broadcasted_iota(jnp.int32, (slots, elements), 0) + faces
            for f in range(4):
                source = source_ref[f : f + 1, :]
                lanes = slice(f * elements, (f + 1) * elements)
                hot_local[:, lanes] = jnp.where(local_row == source, 1.0, 0.0).astype(BF16)
                hot_ghost[:, lanes] = jnp.where(ghost_row == source, 1.0, 0.0).astype(BF16)
            ratio = jnp.where(curved_ref[...] == 1, ratio_ref[...], 1.0)
            scale[...] = jnp.where(alive, ratio, 0.0)
            deriv = deriv_ref[...].reshape(3 * NODES, NODES)
            deriv_high, deriv_low = halves(deriv)
            lift_parts = jnp.concatenate([x.astype(F32) for x in halves(lift_raw[...])], axis=0)
            lift_ref[...] = dot(lift_parts.astype(BF16), spread_ref[...]).astype(BF16)

        def slope(c):
            high, low = parts[c]
            s = dot(deriv_high, high) + (dot(deriv_low, high) + dot(deriv_high, low))
            return s[0:NODES], s[NODES : 2 * NODES], s[2 * NODES :]

        def along(s, x):
            return (
                metric_ref[x : x + 1, :] * s[0]
                + metric_ref[3 + x : 4 + x, :] * s[1]
                + metric_ref[6 + x : 7 + x, :] * s[2]
            )

        for q in range(2):
            sx, sy, sz = slope(3 * q), slope(3 * q + 1), slope(3 * q + 2)
            curl = (
                along(sz, 1) - along(sy, 2),
                along(sx, 2) - along(sz, 0),
                along(sy, 0) - along(sx, 1),
            )
            for c in range(3):
                if q == 0:
                    volume[3 + c] = curl[c]
                else:
                    volume[c] = -curl[c]
        for f in range(4):
            lanes = slice(f * elements, (f + 1) * elements)
            gathered[:, lanes] = dot(table[...], hot_local[:, lanes])

        for o in range(3):

            def land(o=o):
                for j in peers(o):
                    arrival(step, o, j).wait_recv()

            guarded(recv_ok[o], land)

        ghost_high, ghost_low = halves(ghost[step])
        far_high = dot_nt(unpack_ref[...], ghost_high)
        far_low = dot_nt(unpack_ref[...], ghost_low)
        far = jnp.concatenate(
            [far_high[:GROUP], far_low[:GROUP], far_high[GROUP:], far_low[GROUP:]], axis=0
        ).astype(BF16)

        turn = turn_ref[...]
        flux = [[] for _ in range(6)]
        for f in range(4):
            lanes = slice(f * elements, (f + 1) * elements)
            outer = gathered[:, lanes] + dot(far, hot_ghost[:, lanes])
            symmetry = perm_ref[f : f + 1, :]
            jump = []
            for q in range(2):
                pair = outer[q * PAIR : (q + 1) * PAIR]
                turned = dot(turn, pair.astype(BF16))
                exterior = pair[:GROUP] + pair[GROUP:]
                for p in range(1, 6):
                    exterior = jnp.where(symmetry == p, turned[(p - 1) * GROUP : p * GROUP], exterior)
                difference = exterior - inner[q, f]
                jump += [difference[c * ROWS : (c + 1) * ROWS] for c in range(3)]
            nx, ny, nz = (geom_ref[k, f : f + 1, :] for k in range(3))
            half = 0.5 * geom_ref[3, f : f + 1, :]
            along_h = nx * jump[0] + ny * jump[1] + nz * jump[2]
            along_e = nx * jump[3] + ny * jump[4] + nz * jump[5]
            flux[0].append(half * (nz * jump[4] - ny * jump[5] + jump[0] - along_h * nx))
            flux[1].append(half * (nx * jump[5] - nz * jump[3] + jump[1] - along_h * ny))
            flux[2].append(half * (ny * jump[3] - nx * jump[4] + jump[2] - along_h * nz))
            flux[3].append(half * (ny * jump[2] - nz * jump[1] + jump[3] - along_e * nx))
            flux[4].append(half * (nz * jump[0] - nx * jump[2] + jump[4] - along_e * ny))
            flux[5].append(half * (nx * jump[1] - ny * jump[0] + jump[5] - along_e * nz))
        for c in range(6):
            high, low = halves(jnp.concatenate(flux[c], axis=0))
            if step == 1:
                flux_high[c] = high
                flux_low[c] = low
            else:
                register = TIME_STEP * ((volume[c] + lifted(lift_ref[...], high, low)) * scale[...])
                reg_ref[c] = register
                adv_ref[c] = adv_ref[c] + RK_B[0] * register

    for step in range(2):
        for o in range(3):

            def sent(o=o, step=step):
                for j in peers(o):
                    copy(step, o, j).wait_send()

            guarded(send_ok[o], sent)


def finish(
    adv_ref, reg_ref, volume, scale, flux_high, flux_low, lift_ref, adv_hbm, reg_hbm, adv_out, reg_out, sem
):
    writes = []
    for c in range(6):
        register = TIME_STEP * ((volume[c] + lifted(lift_ref[...], flux_high[c], flux_low[c])) * scale[...])
        register = RK_A[1] * reg_ref[c] + register
        reg_out[c] = register
        adv_out[c] = adv_ref[c] + RK_B[1] * register
        for k, (src, dst) in enumerate(((reg_out, reg_hbm), (adv_out, adv_hbm))):
            write = pltpu.make_async_copy(src.at[c], dst.at[c], sem.at[k, c])
            write.start()
            writes.append(write)
    for write in writes:
        write.wait()


def on_device(
    n_dom,
    n_sub,
    fields,
    metric,
    face_geom,
    jacobian_ratio,
    curved,
    derivatives,
    lift_matrix,
    live_count,
    send_list,
    face_source,
    face_permutation,
):
    elements = fields.shape[2]
    faces = 4 * elements
    slots = 3 * n_sub * send_list.shape[3]
    vmem = pl.BlockSpec(memory_space=pltpu.VMEM)
    hbm = pl.BlockSpec(memory_space=pltpu.HBM)
    pick, spread, turn, pack, unpack = zero_one_matrices()
    operands = (
        fields,
        send_list.reshape(send_list.shape[1:]),
        pick,
        pack,
        face_source,
        derivatives,
        metric,
        curved.reshape(1, elements),
        jacobian_ratio,
        unpack,
        turn,
        face_permutation,
        face_geom,
        lift_matrix,
        spread,
    )
    operands = [pltpu.with_memory_space_constraint(a, pltpu.HBM) for a in operands]
    held = [pltpu.VMEM(a.shape, a.dtype) for a in operands[1:]]
    whole = jax.ShapeDtypeStruct(fields.shape, F32)
    flux = jax.ShapeDtypeStruct((6, 4 * ROWS, elements), BF16)
    carried = pl.pallas_call(
        functools.partial(kernel, n_dom, n_sub),
        out_shape=(
            whole,
            whole,
            whole,
            jax.ShapeDtypeStruct((NODES, elements), F32),
            flux,
            flux,
            jax.ShapeDtypeStruct((2 * NODES, 4 * ROWS), BF16),
        ),
        in_specs=[pl.BlockSpec(memory_space=pltpu.SMEM)] + [hbm] * 15,
        out_specs=(vmem,) * 7,
        scratch_shapes=held
        + [
            pltpu.VMEM((2 * PAIR, faces), BF16),
            pltpu.VMEM((2, 4, GROUP, elements), F32),
            pltpu.VMEM((2 * PAIR, faces), F32),
            pltpu.VMEM((faces, faces), BF16),
            pltpu.VMEM((slots, faces), BF16),
            pltpu.VMEM((slots, faces), BF16),
            pltpu.VMEM((2, slots, LANES), F32),
            pltpu.VMEM((2, slots, LANES), F32),
            pltpu.SemaphoreType.DMA((15,)),
            pltpu.SemaphoreType.DMA((2, 3, n_sub)),
            pltpu.SemaphoreType.DMA((2, 3, n_sub)),
        ],
        compiler_params=pltpu.CompilerParams(
            collective_id=0, has_side_effects=True, vmem_limit_bytes=40 * 1024 * 1024
        ),
        cost_estimate=pl.CostEstimate(flops=4_000_000_000, bytes_accessed=2_000_000, transcendentals=0),
    )(live_count, *operands)
    return pl.pallas_call(
        finish,
        out_shape=(whole, whole),
        in_specs=[vmem] * 7,
        out_specs=(hbm, hbm),
        scratch_shapes=[
            pltpu.VMEM(fields.shape, F32),
            pltpu.VMEM(fields.shape, F32),
            pltpu.SemaphoreType.DMA((2, 6)),
        ],
        compiler_params=pltpu.CompilerParams(vmem_limit_bytes=40 * 1024 * 1024),
        cost_estimate=pl.CostEstimate(flops=100_000_000, bytes_accessed=2_000_000, transcendentals=0),
    )(*carried)


def solution(mesh):
    return jax.shard_map(
        functools.partial(on_device, mesh.shape["dom"], mesh.shape["sub"]),
        mesh=mesh,
        in_specs=(
            P(None, None, ("dom", "sub")),
            P(None, ("dom", "sub")),
            P(None, None, ("dom", "sub")),
            P(None, ("dom", "sub")),
            P(("dom", "sub")),
            P(),
            P(),
            P(("dom", "sub")),
            P(("dom", "sub"), None, None, None),
            P(None, ("dom", "sub")),
            P(None, ("dom", "sub")),
        ),
        out_specs=(P(None, None, ("dom", "sub")), P(None, None, ("dom", "sub"))),
        check_vma=False,
    )
```

profile of v0, /device:TPU:1, one launch (start us, length us, event | category | flops | bytes accessed | tf_op | source)
XLA Modules:
  0.0 16.7 jit_solution(16636078592265721082)
XLA Ops:
  1.3 14.3 %shard_map.167 = (f32[6,56,256]{2,1,0:T(8,128)S(1)}, f32[6,56,256]{2,1,0:T(8,128)S(1)}, f32[6,56,256]{2,1,0:T(8,128)S(1)}, f32[56,256]{1,0:T(8,128)S(1)}, bf16[6...) custom-call(s32[1]{0:T(128)S(6)} %copy.18.live_ref, ...), custom_call_target="tpu_custom_call" | custom-call | flops 4000000000 | bytes 2000000 | tf_op jit(solution)/shard_map/pallas_call | solution.py:448
  15.6 1.1 %shard_map.168 = (f32[6,56,256]{2,1,0:T(8,128)}, f32[6,56,256]{2,1,0:T(8,128)}) custom-call(f32[6,56,256]{2,1,0:T(8,128)S(1)} %get-tuple-element.9.adv_ref, f32[6,56,256]{2,1,0:T(8,128)S(1)} %get-tuple-element.10.reg_ref, f32[6,56,256]{2,1,0:T(8,128)S(1)} %get-tuple-element.11.volume, f32[56,256]{1,0:T(8,128)S(1)} %get-tuple-element.12.scale, ...), custom_call_target="tpu_custom_call" | custom-call | flops 100000000 | bytes 2000000 | tf_op jit(solution)/shard_map/pallas_call | solution.py:480
where the time goes:
time: 16.8 us; the launch traced here: 16.7 us
  Pallas kernels  15.4 us (92%)
  between operations  1.29 us (8%)
    pallas_call x1, Pallas kernels, on_device(): pl.pallas_call(functools.partial(kernel, n_dom, n_sub), out_shape=(whole,...  14.3 us
    pallas_call x1, Pallas kernels, on_device(): pl.pallas_call(finish, out_shape=(whole, whole), in_specs=[vmem] * 7, out...  1.12 us

commit v1 on v0

--- a/solution.py
+++ b/solution.py
@@ -61,7 +61,7 @@
             for m in range(TRACE):
                 for part in range(2):
                     turn[(p - 1) * GROUP + c * ROWS + m, part * GROUP + c * ROWS + permuted[p, m]] = 1
-    pack = np.zeros((2 * PAIR, LANES), np.float32)
+    pack = np.zeros((LANES, 2 * PAIR), np.float32)
     unpack = np.zeros((2 * GROUP, LANES), np.float32)
     for q in range(2):
         for c in range(3):
@@ -69,7 +69,7 @@
                 lane = (3 * q + c) * TRACE + m
                 unpack[q * GROUP + c * ROWS + m, lane] = 1
                 for part in range(2):
-                    pack[q * PAIR + part * GROUP + c * ROWS + m, lane] = 1
+                    pack[lane, q * PAIR + part * GROUP + c * ROWS + m] = 1
     return tuple(jnp.asarray(a, BF16) for a in (pick, spread, turn, pack, unpack))
 
 
@@ -138,6 +138,7 @@
     hot_local,
     hot_ghost,
     hot_send,
+    send_row,
     out_buf,
     ghost,
     load_sem,
@@ -166,8 +167,8 @@
             )
         )
     ]
-    for load in loads:
-        load.start()
+    for i in (1, 0, 2, 3, *range(4, len(loads))):
+        loads[i].start()
     elements = adv_ref.shape[2]
     faces = 4 * elements
     cap = send_ref.shape[2]
@@ -221,16 +222,13 @@
         )
 
     loads[1].wait()
-    square_r = lax.broadcasted_iota(jnp.int32, (cap, cap), 0)
-    square_c = lax.broadcasted_iota(jnp.int32, (cap, cap), 1)
-    face_lane = lax.broadcasted_iota(jnp.int32, (cap, faces), 1)
+    send_row[...] = jnp.full(send_row.shape, -1, jnp.int32)
     for o in range(3):
         for j in range(n_sub):
-            row = send_ref[o, j : j + 1, :]
-            column = jnp.sum(jnp.where(square_r == square_c, row, 0), axis=1, keepdims=True)
             at = (o * n_sub + j) * cap
-            hot_send[at : at + cap, :] = jnp.where(face_lane == column, 1.0, 0.0).astype(BF16)
-
+            send_row[:, at : at + cap] = send_ref[o, j : j + 1, :]
+    face_row = lax.broadcasted_iota(jnp.int32, hot_send.shape, 0)
+    hot_send[...] = jnp.where(face_row == send_row[...], 1.0, 0.0).astype(BF16)
     for load in (loads[0], loads[2], loads[3]):
         load.wait()
     alive = lax.broadcasted_iota(jnp.int32, (1, elements), 1) < live_ref[0]
@@ -256,8 +254,8 @@
                 table[q * PAIR : (q + 1) * PAIR, f * elements : (f + 1) * elements] = jnp.concatenate(
                     [h, l], axis=0
                 ).astype(BF16)
-        outgoing = dot_nt(hot_send[...], table[...])
-        out_buf[step] = dot(outgoing.astype(BF16), pack_ref[...])
+        outgoing = dot(table[...], hot_send[...])
+        out_buf[step] = dot(pack_ref[...], outgoing.astype(BF16)).T
 
         if step == 0:
             for k in range(2):
@@ -421,6 +419,7 @@
     elements = fields.shape[2]
     faces = 4 * elements
     slots = 3 * n_sub * send_list.shape[3]
+    slot_lanes = -(-slots // LANES) * LANES
     vmem = pl.BlockSpec(memory_space=pltpu.VMEM)
     hbm = pl.BlockSpec(memory_space=pltpu.HBM)
     pick, spread, turn, pack, unpack = zero_one_matrices()
@@ -465,8 +464,9 @@
             pltpu.VMEM((2 * PAIR, faces), F32),
             pltpu.VMEM((faces, faces), BF16),
             pltpu.VMEM((slots, faces), BF16),
-            pltpu.VMEM((slots, faces), BF16),
-            pltpu.VMEM((2, slots, LANES), F32),
+            pltpu.VMEM((faces, slot_lanes), BF16),
+            pltpu.VMEM((1, slot_lanes), jnp.int32),
+            pltpu.VMEM((2, slot_lanes, LANES), F32),
             pltpu.VMEM((2, slots, LANES), F32),
             pltpu.SemaphoreType.DMA((15,)),
             pltpu.SemaphoreType.DMA((2, 3, n_sub)),

time: 16.8 us -> 17.3 us (1.030)
  Pallas kernels: 15.4 us -> 15.9 us
    pallas_call x1, Pallas kernels: 14.3 us -> 14.8 us  [on_device(): pl.pallas_call(functools.partial(kernel, n_dom, n_sub), out_shape=(whole,...]
where the time goes in v1:
time: 17.3 us; the launch traced here: 17.2 us
  Pallas kernels  15.9 us (92%)
  between operations  1.29 us (7%)
    pallas_call x1, Pallas kernels, on_device(): pl.pallas_call(functools.partial(kernel, n_dom, n_sub), out_shape=(whole,...  14.8 us
    pallas_call x1, Pallas kernels, on_device(): pl.pallas_call(finish, out_shape=(whole, whole), in_specs=[vmem] * 7, out...  1.12 us

profile of v1, /device:TPU:1, one launch (start us, length us, event | category | flops | bytes accessed | tf_op | source)
XLA Modules:
  0.0 17.2 jit_solution(13673623524972572844)
XLA Ops:
  1.3 14.8 %shard_map.167 = (f32[6,56,256]{2,1,0:T(8,128)S(1)}, f32[6,56,256]{2,1,0:T(8,128)S(1)}, f32[6,56,256]{2,1,0:T(8,128)S(1)}, f32[56,256]{1,0:T(8,128)S(1)}, bf16[6...) custom-call(s32[1]{0:T(128)S(6)} %copy.18.live_ref, ...), custom_call_target="tpu_custom_call" | custom-call | flops 4000000000 | bytes 2000000 | tf_op jit(solution)/shard_map/pallas_call | solution.py:447
  16.0 1.1 %shard_map.168 = (f32[6,56,256]{2,1,0:T(8,128)}, f32[6,56,256]{2,1,0:T(8,128)}) custom-call(f32[6,56,256]{2,1,0:T(8,128)S(1)} %get-tuple-element.9.adv_ref, f32[6,56,256]{2,1,0:T(8,128)S(1)} %get-tuple-element.10.reg_ref, f32[6,56,256]{2,1,0:T(8,128)S(1)} %get-tuple-element.11.volume, f32[56,256]{1,0:T(8,128)S(1)} %get-tuple-element.12.scale, ...), custom_call_target="tpu_custom_call" | custom-call | flops 100000000 | bytes 2000000 | tf_op jit(solution)/shard_map/pallas_call | solution.py:480

commit v2 on v0

--- a/solution.py
+++ b/solution.py
@@ -166,8 +166,8 @@
             )
         )
     ]
-    for load in loads:
-        load.start()
+    for i in (1, 4, 0, 2, 3, *range(5, len(loads))):
+        loads[i].start()
     elements = adv_ref.shape[2]
     faces = 4 * elements
     cap = send_ref.shape[2]
@@ -231,6 +231,14 @@
             at = (o * n_sub + j) * cap
             hot_send[at : at + cap, :] = jnp.where(face_lane == column, 1.0, 0.0).astype(BF16)
 
+    loads[4].wait()
+    local_row = lax.broadcasted_iota(jnp.int32, (faces, elements), 0)
+    ghost_row = lax.broadcasted_iota(jnp.int32, (slots, elements), 0) + faces
+    for f in range(4):
+        source = source_ref[f : f + 1, :]
+        lanes = slice(f * elements, (f + 1) * elements)
+        hot_local[:, lanes] = jnp.where(local_row == source, 1.0, 0.0).astype(BF16)
+        hot_ghost[:, lanes] = jnp.where(ghost_row == source, 1.0, 0.0).astype(BF16)
     for load in (loads[0], loads[2], loads[3]):
         load.wait()
     alive = lax.broadcasted_iota(jnp.int32, (1, elements), 1) < live_ref[0]
@@ -282,25 +290,22 @@
         ghost[step, rows(1, me), :] = out_buf[step, rows(1, me), :]
 
         if step == 0:
-            for load in loads[4:]:
+            for load in loads[5:]:
                 load.wait()
-            local_row = lax.broadcasted_iota(jnp.int32, (faces, elements), 0)
-            ghost_row = lax.broadcasted_iota(jnp.int32, (slots, elements), 0) + faces
-            for f in range(4):
-                source = source_ref[f : f + 1, :]
-                lanes = slice(f * elements, (f + 1) * elements)
-                hot_local[:, lanes] = jnp.where(local_row == source, 1.0, 0.0).astype(BF16)
-                hot_ghost[:, lanes] = jnp.where(ghost_row == source, 1.0, 0.0).astype(BF16)
             ratio = jnp.where(curved_ref[...] == 1, ratio_ref[...], 1.0)
             scale[...] = jnp.where(alive, ratio, 0.0)
             deriv = deriv_ref[...].reshape(3 * NODES, NODES)
             deriv_high, deriv_low = halves(deriv)
+            deriv_parts = jnp.concatenate(
+                [deriv_high.astype(F32), deriv_low.astype(F32)], axis=0
+            ).astype(BF16)
             lift_parts = jnp.concatenate([x.astype(F32) for x in halves(lift_raw[...])], axis=0)
             lift_ref[...] = dot(lift_parts.astype(BF16), spread_ref[...]).astype(BF16)
 
         def slope(c):
             high, low = parts[c]
-            s = dot(deriv_high, high) + (dot(deriv_low, high) + dot(deriv_high, low))
+            main = dot(deriv_parts, high)
+            s = main[: 3 * NODES] + (main[3 * NODES :] + dot(deriv_high, low))
             return s[0:NODES], s[NODES : 2 * NODES], s[2 * NODES :]
 
         def along(s, x):

time: 16.8 us -> 17.2 us (1.024)
  Pallas kernels: 15.4 us -> 15.7 us
    pallas_call x1, Pallas kernels: 14.3 us -> 14.6 us  [on_device(): pl.pallas_call(functools.partial(kernel, n_dom, n_sub), out_shape=(whole,...]
where the time goes in v2:
time: 17.2 us; the launch traced here: 17 us
  Pallas kernels  15.7 us (91%)
  between operations  1.29 us (8%)
    pallas_call x1, Pallas kernels, on_device(): pl.pallas_call(functools.partial(kernel, n_dom, n_sub), out_shape=(whole,...  14.6 us
    pallas_call x1, Pallas kernels, on_device(): pl.pallas_call(finish, out_shape=(whole, whole), in_specs=[vmem] * 7, out...  1.12 us

profile of v2, /device:TPU:1, one launch (start us, length us, event | category | flops | bytes accessed | tf_op | source)
XLA Modules:
  0.0 17.0 jit_solution(14252517178772194624)
XLA Ops:
  1.3 14.6 %shard_map.167 = (f32[6,56,256]{2,1,0:T(8,128)S(1)}, f32[6,56,256]{2,1,0:T(8,128)S(1)}, f32[6,56,256]{2,1,0:T(8,128)S(1)}, f32[56,256]{1,0:T(8,128)S(1)}, bf16[6...) custom-call(s32[1]{0:T(128)S(6)} %copy.18.live_ref, ...), custom_call_target="tpu_custom_call" | custom-call | flops 4000000000 | bytes 2000000 | tf_op jit(solution)/shard_map/pallas_call | solution.py:453
  15.9 1.1 %shard_map.168 = (f32[6,56,256]{2,1,0:T(8,128)}, f32[6,56,256]{2,1,0:T(8,128)}) custom-call(f32[6,56,256]{2,1,0:T(8,128)S(1)} %get-tuple-element.9.adv_ref, f32[6,56,256]{2,1,0:T(8,128)S(1)} %get-tuple-element.10.reg_ref, f32[6,56,256]{2,1,0:T(8,128)S(1)} %get-tuple-element.11.volume, f32[56,256]{1,0:T(8,128)S(1)} %get-tuple-element.12.scale, ...), custom_call_target="tpu_custom_call" | custom-call | flops 100000000 | bytes 2000000 | tf_op jit(solution)/shard_map/pallas_call | solution.py:485
